TPU v7x, 128 devices: a whole 4x4x4 slice. The times are simulated.
128 devices in a mesh: dp: 4 (over x), seq: 32 (over z, y, core).
Axes of the slice: x: 4, y: 4, z: 4, core: 2. Of those that a mesh axis runs over, the one named last changes fastest.
Arguments:
- ssm_input: bfloat16 [4, 8192, 3072], P('dp', 'seq'), may hold values from -6 to 6
- gate_input: bfloat16 [4, 8192, 3072], P('dp', 'seq'), may hold values from -6 to 6
- input_map: bfloat16 [4, 8192, 128], P('dp', 'seq'), may hold values from -0.52734375 to 0.52734375
- output_map: bfloat16 [4, 8192, 128], P('dp', 'seq'), may hold values from -6 to 6
- step_logit: bfloat16 [4, 8192, 48], P('dp', 'seq'), may hold values from -5 to 5
- step_bias: float32 [48], replicated, may hold values from -1 to 1
- decay_rate: float32 [48], replicated, may hold values from 6.1035156e-07 to 0.05
- skip_gain: float32 [48], replicated, may hold values from 0.5 to 1.5
- norm_gain: float32 [3072], replicated, may hold values from 0.1 to 1.9
- out_weight: bfloat16 [3072, 1536], replicated, may hold values from -0.109375 to 0.109375
- resets: int32 [4, 4], P('dp'), may hold values from 1 to 8191
- out_grad: bfloat16 [4, 8192, 1536], P('dp', 'seq'), may hold values from -6 to 6
Outputs:
- mixed_out: bfloat16 [4, 8192, 1536], P('dp', 'seq')
- grad_input: bfloat16 [4, 8192, 3072], P('dp', 'seq')
- grad_gate: bfloat16 [4, 8192, 3072], P('dp', 'seq')
- grad_inmap: bfloat16 [4, 8192, 128], P('dp', 'seq')
- grad_outmap: bfloat16 [4, 8192, 128], P('dp', 'seq')
- grad_step: bfloat16 [4, 8192, 48], P('dp', 'seq')
- grad_bias: float32 [48], replicated
- grad_rate: float32 [48], replicated
- grad_skip: float32 [48], replicated
- grad_gain: float32 [3072], replicated
- grad_weight: float32 [3072, 1536], P('seq')
All inputs are finite; a program needn't handle non-finite values.
Results may differ from a plain program's by a relative error of at most 0.0049.
Values sent between devices are 32-bit elements; how exact they have to be, the bound alone decides.
A program may use at most 384 MiB of HBM per device.

v0:
```python
import jax
import jax.numpy as jnp
from jax import lax
from jax.sharding import PartitionSpec as P

SPAN = 128
highest = lax.Precision.HIGHEST


def prefix(shard, axis, combine, identity, reverse):
    count, place = (lax.axis_size(axis), lax.axis_index(axis))
    everything = jax.tree.map(lambda part: lax.all_gather(part, axis), shard)
    start = jax.tree.map(
        lambda part, zero: jnp.broadcast_to(jnp.asarray(zero, part.dtype), part.shape),
        shard,
        identity,
    )

    def hop(k, before):
        at = count - 1 - k if reverse else k
        reached = at > place if reverse else at < place
        new = combine(before, jax.tree.map(lambda part: part[at], everything))
        return jax.tree.map(lambda a, b: jnp.where(reached, a, b), new, before)

    return lax.fori_loop(0, count, hop, start)


def block_step(state_in, inputs):
    x_blk, b_blk, c_blk, step_blk, decay_blk, flag_blk = inputs
    cumulative = jnp.cumsum(decay_blk, axis=0)
    counts = jnp.cumsum(flag_blk)
    block_len = flag_blk.shape[0]
    row_ids = lax.broadcasted_iota(jnp.int32, (block_len, block_len), 0)
    col_ids = lax.broadcasted_iota(jnp.int32, (block_len, block_len), 1)
    in_mask = ((row_ids >= col_ids) & (counts[:, None] == counts[None, :]))[:, :, None]
    gap_vals = cumulative[:, None, :] - cumulative[None, :, :]
    decay_mat = jnp.where(in_mask, jnp.exp(jnp.where(in_mask, gap_vals, 0.0)), 0.0)
    gram_mat = jnp.einsum("in,jn->ij", c_blk, b_blk, precision=highest)
    mixing = gram_mat[:, :, None] * decay_mat * step_blk[None, :, :]
    y_blk = jnp.einsum("ijh,jhp->ihp", mixing, x_blk, precision=highest)
    opened = (counts == 0)[:, None]
    from_start = jnp.where(opened, jnp.exp(jnp.where(opened, cumulative, 0.0)), 0.0)
    y_blk = y_blk + from_start[:, :, None] * jnp.einsum(
        "in,hpn->ihp", c_blk, state_in, precision=highest
    )
    keep_mask = (counts == counts[-1])[:, None]
    tail_weights = (
        jnp.where(
            keep_mask, jnp.exp(jnp.where(keep_mask, cumulative[-1][None, :] - cumulative, 0.0)), 0.0
        )
        * step_blk
    )
    whole_decay = jnp.where(counts[-1] == 0, jnp.exp(cumulative[-1]), 0.0)
    new_state = whole_decay[:, None, None] * state_in + jnp.einsum(
        "jhp,jn->hpn", tail_weights[:, :, None] * x_blk, b_blk, precision=highest
    )
    return (new_state, y_blk)


def ssd_blocks(x_heads, b_float, c_float, step_vals, log_decay, flags, state_in):
    num_blocks = x_heads.shape[0] // SPAN

    def to_blocks(values):
        return values.reshape((num_blocks, SPAN) + values.shape[1:])

    final_state, y_blocks = lax.scan(
        block_step,
        state_in,
        (
            to_blocks(x_heads),
            to_blocks(b_float),
            to_blocks(c_float),
            to_blocks(step_vals),
            to_blocks(log_decay),
            to_blocks(flags),
        ),
    )
    return (final_state, y_blocks.reshape(x_heads.shape))


def gate_norm(y_ssd, x_float, z_float, skip_gain, norm_gain):
    num_heads = skip_gain.shape[0]
    rows_here = x_float.shape[0]
    y_full = y_ssd.reshape(rows_here, -1) + (
        x_float.reshape(rows_here, num_heads, -1) * skip_gain[None, :, None]
    ).reshape(x_float.shape)
    gated_vals = y_full * jax.nn.silu(z_float)
    scale_inv = lax.rsqrt(jnp.mean(gated_vals * gated_vals, axis=-1, keepdims=True) + 1e-05)
    return gated_vals * scale_inv * norm_gain


def step_sizes(logit_vals, bias_in, rate_in):
    step_vals = jax.nn.softplus(logit_vals + bias_in)
    return (step_vals, -rate_in * step_vals)


def combine(earlier, later):
    return (earlier[0] * later[0], later[0][:, None, None] * earlier[1] + later[1])


def per_device(
    ssm_input,
    gate_input,
    input_map,
    output_map,
    step_logit,
    step_bias,
    decay_rate,
    skip_gain,
    norm_gain,
    out_weight,
    resets,
    out_grad,
):
    rows_here = ssm_input.shape[1]
    num_heads = step_bias.shape[0]
    x_float = ssm_input[0].astype(jnp.float32)
    z_float = gate_input[0].astype(jnp.float32)
    b_float = input_map[0].astype(jnp.float32)
    c_float = output_map[0].astype(jnp.float32)
    logit_float = step_logit[0].astype(jnp.float32)
    inner_width = x_float.shape[1]
    head_size = inner_width // num_heads
    x_heads = x_float.reshape(rows_here, num_heads, head_size)
    positions = lax.axis_index("seq") * rows_here + lax.iota(jnp.int32, rows_here)
    flags = jnp.max((positions[:, None] == resets[0][None, :]).astype(jnp.int32), axis=1)
    counts = jnp.cumsum(flags)
    opened = (counts == 0)[:, None]
    clean_shard = counts[-1] == 0
    empty_state = jnp.zeros((num_heads, head_size, b_float.shape[1]), jnp.float32)
    identity = (jnp.ones((num_heads,), jnp.float32), empty_state)
    step_vals, log_decay = step_sizes(logit_float, step_bias, decay_rate)
    cumulative = jnp.cumsum(log_decay, axis=0)
    from_start = jnp.where(opened, jnp.exp(jnp.where(opened, cumulative, 0.0)), 0.0)
    shard_through = jnp.where(clean_shard, jnp.exp(cumulative[-1]), 0.0)
    step_vals, cumulative, from_start, through = (step_vals, cumulative, from_start, shard_through)
    keep_mask = (counts == counts[-1])[:, None]
    tail_weights = (
        jnp.where(
            keep_mask, jnp.exp(jnp.where(keep_mask, cumulative[-1][None, :] - cumulative, 0.0)), 0.0
        )
        * step_vals
    )
    shard_state = jnp.einsum(
        "thp,tn->hpn", tail_weights[:, :, None] * x_heads, b_float, precision=highest
    )
    incoming = prefix((through, shard_state), "seq", combine, identity, False)[1]

    def from_incoming(x_part, b_part, c_part, logit_vals, bias_in, rate_in):
        step_part, decay_part = step_sizes(logit_vals, bias_in, rate_in)
        return ssd_blocks(x_part, b_part, c_part, step_part, decay_part, flags, incoming)

    (final_state, y_ssd), ssd_pullback = jax.vjp(
        from_incoming, x_heads, b_float, c_float, logit_float, step_bias, decay_rate
    )
    normed_f, post_pullback = jax.vjp(gate_norm, y_ssd, x_float, z_float, skip_gain, norm_gain)
    normed = normed_f.astype(jnp.bfloat16)
    mixed = jnp.dot(normed, out_weight, preferred_element_type=jnp.float32).astype(jnp.bfloat16)
    grad_rows = out_grad[0]
    normed_grad = lax.dot_general(
        grad_rows, out_weight, (((1,), (1,)), ((), ())), preferred_element_type=jnp.float32
    )
    y_grad, x_grad_skip, z_grad, skip_grad, gain_grad = post_pullback(normed_grad)
    start_grad = jnp.einsum(
        "thp,tn->hpn", from_start[:, :, None] * y_grad, c_float, precision=highest
    )
    later_grad = prefix((through, start_grad), "seq", combine, identity, True)[1]
    x_grad, b_grad, c_grad, logit_grad, bias_grad, rate_grad = ssd_pullback((later_grad, y_grad))
    bias_sum, rate_sum, skip_sum, gain_sum = lax.psum(
        (bias_grad, rate_grad, skip_grad, gain_grad), ("dp", "seq")
    )
    seq_rows = lax.psum_scatter(
        lax.dot_general(
            normed, grad_rows, (((0,), (0,)), ((), ())), preferred_element_type=jnp.float32
        ),
        "seq",
        scatter_dimension=0,
        tiled=True,
    )
    weight_grad = lax.psum(seq_rows, "dp")
    grad_input = (x_grad.reshape(rows_here, inner_width) + x_grad_skip).astype(jnp.bfloat16)
    return (
        mixed[None],
        grad_input[None],
        z_grad.astype(jnp.bfloat16)[None],
        b_grad.astype(jnp.bfloat16)[None],
        c_grad.astype(jnp.bfloat16)[None],
        logit_grad.astype(jnp.bfloat16)[None],
        bias_sum,
        rate_sum,
        skip_sum,
        gain_sum,
        weight_grad,
    )


def solution(mesh):
    placed = (
        P("dp", "seq", None),
        P("dp", "seq", None),
        P("dp", "seq", None),
        P("dp", "seq", None),
        P("dp", "seq", None),
        P(),
        P(),
        P(),
        P(),
        P(),
        P("dp", None),
        P("dp", "seq", None),
    )
    return jax.shard_map(
        per_device,
        mesh=mesh,
        in_specs=placed,
        out_specs=(
            P("dp", "seq", None),
            P("dp", "seq", None),
            P("dp", "seq", None),
            P("dp", "seq", None),
            P("dp", "seq", None),
            P("dp", "seq", None),
            P(),
            P(),
            P(),
            P(),
            P("seq", None),
        ),
        check_vma=False,
    )
```

profile of v0, /device:TPU:1, one launch (start us, length us, event | category | flops | bytes accessed | tf_op | source)
XLA Modules:
  0.0 973.6 jit_solution(15452090480564412764)
XLA Ops:
  17.8 3.7 copy.144
  21.5 4.1 convert_multiply_fusion
  25.6 3.6 copy.145
  29.2 4.5 fusion.162
  34.0 3.1 copy.147
  37.1 5.3 reshape.1003
  42.5 4.0 copy.148
  46.5 3.2 copy.152
  49.7 5.5 reshape.1008
  55.9 24.0 %all-gather.2 = f32[32,1,48]{2,1,0:T(1,128)S(1)} all-gather(f32[1,1,48]{2,1,0:T(1,128)S(1)} %bitcast.581), channel_id=1, replica_groups=mesh['dp'=4,'seq'=32] {'seq'}, dimensions={0}, use_global_device_ids=true | all-gather | bytes 6336 | tf_op jit(solution)/shard_map/all_gather | solution.py:12
  79.9 115.2 %all-gather.6.cloned.1.call-done = f32[1536,64,128]{2,1,0:T(8,128)} async-done(((f32[48,64,128]{2,1,0:T(8,128)}), f32[1536,64,128]{2,1,0:T(8,128)}) %all-gather.6.cloned.1.call-update) | async-done | bytes 50331664 | tf_op jit(solution)/shard_map/all_gather | solution.py:12
  195.1 58.0 %while.116 = (s32[]{:T(128)}, f32[48,64,128]{2,1,0:T(8,128)S(1)}, s32[]{:T(128)}, f32[32,48]{1,0:T(8,128)S(1)}, f32[32,48,64,128]{3,2,1,0:T(8,128)}, /*index=5*/s32[]{:T(128)}, s32[]{:T(128)}) while((s32[]{:T(128)}, f32[48,64,128]{2,1,0:T(8,128)S(1)}, s32[]{:T(128)}, f32[32,48]{1,0:T(8,128)S(1)}, f32[32,48,64,128]{3,2,1,0:T(8,128)}, ...), condition=%wide.region_6.7_spmd.clone, body=%wide.region_5.6_spmd.clone.sunk | while | flops 1572868 | bytes 4719273 | solution.py:25
  259.2 154.5 %while.115 = (s32[]{:T(128)}, f32[48,64,128]{2,1,0:T(8,128)S(1)}, f32[2,128,48,64]{1,3,2,0:T(8,128)}, pred[2,128,128,48]{2,1,3,0:T(32,128)(4,1)}, f32[2,128,128,...) while((s32[]{:T(128)}, f32[48,64,128]{2,1,0:T(8,128)S(1)}, ...), condition=%wide.region_10.11_spmd.clone, body=%wide.region_7.10_spmd.clone.sunk | while | flops 1848273152 | bytes 111490832 | solution.py:66
  262.9 11.3 %broadcast_multiply_fusion.4 = (f32[1,128,128,48]{3,2,1,0:T(8,128)}, f32[1,128,128,48]{3,2,1,0:T(8,128)}, f32[1,128,128,48]{3,2,1,0:T(8,128)}, f32[1,128,128,48]{3,2,1,0:T(8,128)}) fusion(f32[128,48]{1,0:T(8,128)S(1)} %get-tuple-element.2450, f32[128,48]{1,0:T(8,128)S(1)} %reduce_window_sum.92, pred[128,128]{1,0:T(8,128)(4,1)S(1)} %fusion.251, ...), kind=kLoop, calls=%fused_computation.99.clone.1 | loop fusion | flops 3932160 | bytes 12713984 | tf_op jit(solution)/shard_map/jvp()/while/body/eval_jaxpr/mul | solution.py:39
  274.2 6.9 copy.272
  281.1 6.8 copy.273
  287.9 6.3 constant_dynamic-update-slice_fusion.23
  294.2 6.9 copy.269
  301.1 6.8 copy.270
  307.9 6.4 constant_dynamic-update-slice_fusion.21
  314.5 2.6 bitcast_dynamic-update-slice_fusion.11
  317.1 7.6 bitcast_dynamic-update-slice_fusion.13
  324.7 2.9 multiply_dynamic-update-slice_fusion.2
  339.9 11.3 %broadcast_multiply_fusion.4 = (f32[1,128,128,48]{3,2,1,0:T(8,128)}, f32[1,128,128,48]{3,2,1,0:T(8,128)}, f32[1,128,128,48]{3,2,1,0:T(8,128)}, f32[1,128,128,48]{3,2,1,0:T(8,128)}) fusion(f32[128,48]{1,0:T(8,128)S(1)} %get-tuple-element.2450, f32[128,48]{1,0:T(8,128)S(1)} %reduce_window_sum.92, pred[128,128]{1,0:T(8,128)(4,1)S(1)} %fusion.251, ...), kind=kLoop, calls=%fused_computation.99.clone.1 | loop fusion | flops 3932160 | bytes 12713984 | tf_op jit(solution)/shard_map/jvp()/while/body/eval_jaxpr/mul | solution.py:39
  351.2 6.9 copy.272
  358.1 6.8 copy.273
  365.0 6.3 constant_dynamic-update-slice_fusion.23
  371.2 6.9 copy.269
  378.1 6.8 copy.270
  384.9 6.4 constant_dynamic-update-slice_fusion.21
  391.6 2.6 bitcast_dynamic-update-slice_fusion.11
  394.2 7.6 bitcast_dynamic-update-slice_fusion.13
  401.8 2.9 multiply_dynamic-update-slice_fusion.2
  413.7 7.7 multiply_reduce_fusion.2
  421.4 3.9 multiply_convert_fusion
  425.3 7.8 fusion.146
  436.0 3.6 copy.153
  439.6 6.5 copy.180
  446.1 6.4 reshape.1022
  452.5 10.8 %multiply_reduce_fusion = (f32[3072]{0:T(1024)}, f32[256]{0:T(256)S(1)}, f32[256,3072]{1,0:T(8,128)S(1)}) fusion(f32[256]{0:T(256)S(1)} %bitcast_rsqrt_fusion, bf16[1,256,3072]{2,1,0:T(8,128)(2,1)} %param.21, f32[256,3072]{1,0:T(8,128)} %reshape.1022, f32[3072]{0:T(1024)S(1)} %mul.708, bf16[1,256,3072]{2,1,0:T(8,128)(2,1)S(1)} %copy-done.8, ...), kind=kOutput, calls=%fused_computation.207 | convolution fusion | flops 2427712256 | bytes 19699712 | tf_op jit(solution)/shard_map/dot_general | solution.py:160
  463.3 3.9 fusion.142
  471.0 4.1 copy.154
  475.1 4.6 fusion.160
  480.5 6.1 reshape.1023
  486.6 7.1 copy.158
  494.4 10.0 %fusion.143 = bf16[1,256,1536]{2,1,0:T(8,128)(2,1)} fusion(bf16[3072,1536]{1,0:T(8,128)(2,1)} %param.29, f32[3072]{0:T(1024)S(1)} %copy-done.27, f32[256]{0:T(256)S(1)} %bitcast_rsqrt_fusion, f32[256,3072]{1,0:T(8,128)} %reshape.1022, bf16[1,256,3072]{2,1,0:T(8,128)(2,1)} %param.20, f32[3072]{0:T(1024)S(1)} %mul.708, bf16[1,256,3072]{2,1,0:T(8,128)(2,1)} %param.21), kind=kOutput, calls=%fused_computation.213 | convolution fusion | flops 2425749504 | bytes 16540672 | tf_op jit(solution)/shard_map/dot_general | solution.py:158
  504.3 48.3 %reduce-scatter.2.cloned.1.call-done = f32[96,1536]{1,0:T(8,128)} async-done(((f32[3072,1536]{1,0:T(8,128)}), f32[96,1536]{1,0:T(8,128)}) %reduce-scatter.2.cloned.1.call-update) | async-done | bytes 589840 | tf_op jit(solution)/shard_map/reduce_scatter | solution.py:172
  552.7 161.2 %all-gather.8.cloned.1.call-done = f32[1536,64,128]{2,1,0:T(8,128)} async-done(((f32[48,64,128]{2,1,0:T(8,128)}), f32[1536,64,128]{2,1,0:T(8,128)}) %all-gather.8.cloned.1.call-update) | async-done | bytes 50331664 | tf_op jit(solution)/shard_map/all_gather | solution.py:12
  713.8 79.9 %while.117 = (s32[]{:T(128)}, f32[48,64,128]{2,1,0:T(8,128)S(1)}, s32[]{:T(128)}, f32[32,48]{1,0:T(8,128)}, f32[32,48,64,128]{3,2,1,0:T(8,128)}, /*index=5*/s32[]{:T(128)}, s32[]{:T(128)}, s32[]{:T(128)}, s32[]{:T(128)}) while((s32[]{:T(128)}, f32[48,64,128]{2,1,0:T(8,128)S(1)}, s32[]{:T(128)}, f32[32,48]{1,0:T(8,128)}, ...), condition=%wide.region_14.15_spmd.clone, body=%wide.region_13.14_spmd.clone.sunk | while | flops 1572872 | bytes 4719335 | solution.py:25
  797.9 83.0 %while.114 = (s32[]{:T(128)}, f32[48,64,128]{2,1,0:T(8,128)S(1)}, f32[2,128,48,64]{1,3,2,0:T(8,128)}, bf16[2,128,128]{2,1,0:T(8,128)(2,1)}, bf16[2,128,128]{2,1,...) while((s32[]{:T(128)}, f32[48,64,128]{2,1,0:T(8,128)S(1)}, ...), condition=%wide.region_25.26_spmd, body=%wide.region_15.25_spmd.sunk | while | flops 3688450048 | bytes 77251128 | solution.py:66
  798.9 11.1 %fusion.235 = (f32[128,48]{0,1:T(8,128)S(1)}, f32[128,48]{0,1:T(8,128)S(1)}, f32[128,128]{1,0:T(8,128)S(1)}, f32[128,48]{0,1:T(8,128)S(1)}) fusion(f32[2,128,128,48]{2,1,3,0:T(8,128)} %get-tuple-element.2728, s32[]{:T(128)S(6)} %sub.274, f32[128,48]{0,1:T(8,128)S(1)} %dynamic-slice_bitcast_fusion.18, ...), kind=kOutput, calls=%fused_computation.91.clone.1 | convolution fusion | flops 612595712 | bytes 13600256 | tf_op jit(solution)/shard_map/transpose(jvp())/while/body/eval_jaxpr/ijh,jhp->ihp/dot_general | solution.py:40
  812.0 4.0 fusion.233
  821.9 4.7 fusion.237
  827.4 4.0 fusion.234
  831.8 5.5 bitcast_dynamic-update-slice_fusion.10
  840.2 11.1 %fusion.235 = (f32[128,48]{0,1:T(8,128)S(1)}, f32[128,48]{0,1:T(8,128)S(1)}, f32[128,128]{1,0:T(8,128)S(1)}, f32[128,48]{0,1:T(8,128)S(1)}) fusion(f32[2,128,128,48]{2,1,3,0:T(8,128)} %get-tuple-element.2728, s32[]{:T(128)S(6)} %sub.274, f32[128,48]{0,1:T(8,128)S(1)} %dynamic-slice_bitcast_fusion.18, ...), kind=kOutput, calls=%fused_computation.91.clone.1 | convolution fusion | flops 612595712 | bytes 13600256 | tf_op jit(solution)/shard_map/transpose(jvp())/while/body/eval_jaxpr/ijh,jhp->ihp/dot_general | solution.py:40
  853.3 4.0 fusion.233
  863.2 4.7 fusion.237
  868.8 4.0 fusion.234
  873.2 5.4 bitcast_dynamic-update-slice_fusion.10
  883.0 6.1 copy.183
  889.1 5.8 reshape.1024
  895.7 64.7 %all-reduce.2 = (f32[48]{0:T(128)}, f32[48]{0:T(128)}, f32[48]{0:T(128)}, f32[3072]{0:T(1024)}) all-reduce(f32[48]{0:T(128)S(1)} %get-tuple-element.1778, f32[48]{0:T(128)S(1)} %neg.49, f32[48]{0:T(128)S(1)} %copy-done.36, f32[3072]{0:T(1024)S(1)} %copy-done.32), channel_id=1, replica_groups=mesh['dp'=4,'seq'=32] {'dp','seq'}, use_global_device_ids=true, to_apply=%region_27.28 | all-reduce | flops 3216 | bytes 25728 | tf_op jit(solution)/shard_map/psum | solution.py:169
  960.4 4.6 fusion.145
  (449 shorter events, 217.1 us)
Async XLA Ops:
  7.2 418.2 %copy-start = (bf16[1,256,1536]{2,1,0:T(8,128)(2,1)S(1)}, bf16[1,256,1536]{2,1,0:T(8,128)(2,1)}, u32[]{:S(2)}) copy-start(bf16[1,256,1536]{2,1,0:T(8,128)(2,1)} %param.31) | copy-start | bytes 2359300
  7.2 187.9 %all-gather.6.cloned.1.call-start = ((), (), s32[]{:S(2)}) async-start(), calls=%async_computation.3 | async-start | bytes 51904512 | tf_op jit(solution)/shard_map/all_gather | solution.py:12
  12.5 67.4 %copy-start.33 = (f32[48]{0:T(128)}, f32[48]{0:T(128)S(1)}, u32[]{:S(2)}) copy-start(f32[48]{0:T(128)S(1)} %neg.43) | copy-start | bytes 580
  17.8 3.7 copy-start.7
  25.6 3.6 copy-start.16
  29.2 4.6 copy-start.14
  33.8 518.9 %reduce-scatter.2.cloned.1.call-start = ((), (), s32[]{:S(2)}) async-start(), calls=%async_computation.1 | async-start | bytes 19464192 | tf_op jit(solution)/shard_map/reduce_scatter | solution.py:172
  33.9 45.9 %copy-start.12 = (f32[1,256,48]{2,1,0:T(8,128)}, f32[1,256,48]{2,1,0:T(8,128)S(1)}, u32[]{:S(2)}) copy-start(f32[1,256,48]{2,1,0:T(8,128)S(1)} %copy.179) | copy-start | bytes 147460
  42.5 4.0 copy-start.17
  49.7 5.5 copy-start.26
  49.7 30.2 %copy-start.29 = (f32[48]{0:T(128)S(1)}, f32[48]{0:T(128)}, u32[]{:S(2)}) copy-start(f32[48]{0:T(128)} %param.25) | copy-start | bytes 580
  253.1 4.1 copy-start.28
  314.5 2.6 copy-start.2
  328.3 2.5 copy-start.3
  330.7 3.5 copy-start.21
  330.7 3.5 copy-start.40
  330.7 3.6 copy-start.31
  330.7 3.6 copy-start.37
  330.8 4.9 copy-start.43
  334.3 2.2 copy-start.22
  334.3 2.1 copy-start.41
  334.4 2.1 copy-start.38
  335.7 0.7 copy-start.44
  391.6 2.6 copy-start.2
  405.3 2.5 copy-start.3
  407.8 3.5 copy-start.21
  407.8 3.5 copy-start.40
  407.8 3.5 copy-start.31
  407.8 3.6 copy-start.37
  407.8 4.9 copy-start.43
  411.3 2.2 copy-start.22
  411.3 2.1 copy-start.41
  411.4 2.1 copy-start.38
  413.7 7.7 copy-start.20
  433.1 0.8 copy-start.19
  433.2 280.7 %all-gather.8.cloned.1.call-start = ((), (), s32[]{:S(2)}) async-start(), calls=%async_computation.4 | async-start | bytes 51904512 | tf_op jit(solution)/shard_map/all_gather | solution.py:12
  446.1 6.4 copy-start.8
  446.1 6.4 copy-start.27
  452.5 10.8 %copy-start.10 = (f32[256,3072]{1,0:T(8,128)S(1)}, f32[256,3072]{1,0:T(8,128)}, u32[]{:S(2)}) copy-start(f32[256,3072]{1,0:T(8,128)} %reshape.1022) | copy-start | bytes 9437188
  452.5 10.8 %copy-start.11 = (bf16[1,256,3072]{2,1,0:T(8,128)(2,1)S(1)}, bf16[1,256,3072]{2,1,0:T(8,128)(2,1)}, u32[]{:S(2)}) copy-start(bf16[1,256,3072]{2,1,0:T(8,128)(2,1)} %param.21) | copy-start | bytes 4718596
  463.3 5.6 copy-start.9
  467.2 1.6 copy-start.6
  471.0 4.1 copy-start.18
  479.8 485.2 %all-reduce.5.cloned.1.call-start = ((), (), s32[]{:S(2)}) async-start(), calls=%async_computation.2 | async-start | bytes 1179648 | tf_op jit(solution)/shard_map/psum | solution.py:180
  793.7 4.2 copy-start.23
  793.7 4.1 copy-start.39
  793.7 4.1 copy-start.42
  793.7 4.1 copy-start.45
  797.9 84.8 %copy-start.13 = (f32[1,256,48]{2,1,0:T(8,128)S(1)}, f32[1,256,48]{2,1,0:T(8,128)}, u32[]{:S(2)}) copy-start(f32[1,256,48]{2,1,0:T(8,128)} %copy-done.12) | copy-start | bytes 147460
  797.9 84.8 %copy-start.30 = (f32[48]{0:T(128)S(1)}, f32[48]{0:T(128)}, u32[]{:S(2)}) copy-start(f32[48]{0:T(128)} %param.25) | copy-start | bytes 580
  797.9 84.8 %copy-start.34 = (f32[48]{0:T(128)S(1)}, f32[48]{0:T(128)}, u32[]{:S(2)}) copy-start(f32[48]{0:T(128)} %copy-done.33) | copy-start | bytes 580
  798.9 11.2 %copy-start.5 = (f32[2,48,64,128]{3,2,1,0:T(8,128)S(1)}, f32[2,48,64,128]{3,2,1,0:T(8,128)}, u32[]{:S(2)}) copy-start(f32[2,48,64,128]{3,2,1,0:T(8,128)} %get-tuple-element.2715) | copy-start | bytes 9437188 | tf_op jit(solution)/shard_map/transpose(jvp())/while
  821.9 9.6 copy-start.24
  821.9 9.9 %copy-start.1 = (f32[2,128,48,64]{1,3,2,0:T(8,128)S(1)}, f32[2,128,48,64]{1,3,2,0:T(8,128)}, u32[]{:S(2)}) copy-start(f32[2,128,48,64]{1,3,2,0:T(8,128)} %get-tuple-element.2706) | copy-start | bytes 9437188 | tf_op jit(solution)/shard_map/transpose(jvp())/while
  821.9 9.9 %copy-start.4 = (f32[128,48,64]{0,2,1:T(8,128)S(1)}, f32[128,48,64]{0,2,1:T(8,128)}, u32[]{:S(2)}) copy-start(f32[128,48,64]{0,2,1:T(8,128)} %get-tuple-element.2407) | copy-start | bytes 4718596 | tf_op jit(solution)/shard_map/transpose(jvp())/while
  831.8 5.5 copy-start.25
  840.2 11.2 %copy-start.5 = (f32[2,48,64,128]{3,2,1,0:T(8,128)S(1)}, f32[2,48,64,128]{3,2,1,0:T(8,128)}, u32[]{:S(2)}) copy-start(f32[2,48,64,128]{3,2,1,0:T(8,128)} %get-tuple-element.2715) | copy-start | bytes 9437188 | tf_op jit(solution)/shard_map/transpose(jvp())/while
  863.2 9.6 copy-start.24
  863.2 9.9 %copy-start.1 = (f32[2,128,48,64]{1,3,2,0:T(8,128)S(1)}, f32[2,128,48,64]{1,3,2,0:T(8,128)}, u32[]{:S(2)}) copy-start(f32[2,128,48,64]{1,3,2,0:T(8,128)} %get-tuple-element.2706) | copy-start | bytes 9437188 | tf_op jit(solution)/shard_map/transpose(jvp())/while
  863.2 9.9 %copy-start.4 = (f32[128,48,64]{0,2,1:T(8,128)S(1)}, f32[128,48,64]{0,2,1:T(8,128)}, u32[]{:S(2)}) copy-start(f32[128,48,64]{0,2,1:T(8,128)} %get-tuple-element.2407) | copy-start | bytes 4718596 | tf_op jit(solution)/shard_map/transpose(jvp())/while
  873.1 5.4 copy-start.25
  889.1 5.9 copy-start.15
  889.1 6.6 copy-start.32
  889.1 6.6 copy-start.36
  (2 other events, 1.4 us)
Sparse Core Ops, SparseCore 0:
  33.9 161.1 all-gather.5
  433.3 119.3 reduce-scatter.1
  555.8 158.0 all-gather.7
  716.2 40.1 all-reduce.4
where the time goes:
time: 984 us; the launch traced here: 974 us
  waiting for transfers between devices  325 us (33%)
  local copies, waits for them, and re-layouts  220 us (22%)
  other arithmetic  192 us (20%)
  matrix products  128 us (13%)
  blocking collectives  88.7 us (9%)
  between operations  15.1 us (2%)
    all_gather x2, waiting for transfers between devices, prefix(): everything = jax.tree.map(lambda part: lax.all_gather(part, axis), shard)  276 us
    select_n x64, other arithmetic, hop(): return jax.tree.map(lambda a, b: jnp.where(reached, a, b), new, before)  113 us
    dynamic_update_slice x44, local copies, waits for them, and re-layouts, ssd_blocks(): lax.scan(block_step, state_in, (to_blocks(x_heads), to_blocks(b_float), t...  89 us
    psum x1, blocking collectives, per_device(): lax.psum((bias_grad, rate_grad, skip_grad, gain_grad), ('dp', 'seq'))  64.7 us
    reduce_scatter x1, waiting for transfers between devices, per_device(): lax.psum_scatter(lax.dot_general(normed, grad_rows, (((0,), (0,)), ((), (...  48.3 us
    dot_general x6, matrix products, block_step(): y_blk = jnp.einsum('ijh,jhp->ihp', mixing, x_blk, precision=highest)  48.3 us
    all_gather x1, blocking collectives, prefix(): everything = jax.tree.map(lambda part: lax.all_gather(part, axis), shard)  24 us
    mul x2, other arithmetic, block_step(): mixing = gram_mat[:, :, None] * decay_mat * step_blk[None, :, :]  22.6 us
  transfers between devices with their start and end apart: 4, of which 3 were waited for; matrix products, arithmetic and copies ran while one was open for 28% of the time, Pallas kernels for 0%

commit v1 on v0

--- a/solution.py
+++ b/solution.py
@@ -167,7 +167,7 @@
     later_grad = prefix((through, start_grad), "seq", combine, identity, True)[1]
     x_grad, b_grad, c_grad, logit_grad, bias_grad, rate_grad = ssd_pullback((later_grad, y_grad))
     bias_sum, rate_sum, skip_sum, gain_sum = lax.psum(
-        (bias_grad, rate_grad, skip_grad, gain_grad), ("dp", "seq")
+        lax.psum((bias_grad, rate_grad, skip_grad, gain_grad), "dp"), "seq"
     )
     seq_rows = lax.psum_scatter(
         lax.dot_general(

time: 984 us -> 1060 us (1.077)
  blocking collectives: 88.7 us -> 159 us
    psum x1 -> x2, blocking collectives: 64.7 us -> 135 us  [the longest x1 122 us: per_device(): lax.psum(lax.psum((bias_grad, rate_grad, skip_grad, gain_grad), 'dp'), 's...]
  transfers between devices with their start and end apart: 4 -> 4, of which waited for: 3 -> 3; matrix products, arithmetic and copies ran while one was open for 28% -> 26% of each run, Pallas kernels for 0% -> 0%
where the time goes in v1:
time: 1060 us; the launch traced here: 1040 us
  waiting for transfers between devices  325 us (31%)
  local copies, waits for them, and re-layouts  220 us (21%)
  other arithmetic  192 us (18%)
  blocking collectives  159 us (15%)
  matrix products  128 us (12%)
  between operations  15.1 us (1%)
    all_gather x2, waiting for transfers between devices, prefix(): everything = jax.tree.map(lambda part: lax.all_gather(part, axis), shard)  276 us
    psum x1, blocking collectives, per_device(): lax.psum(lax.psum((bias_grad, rate_grad, skip_grad, gain_grad), 'dp'), 's...  122 us
    select_n x64, other arithmetic, hop(): return jax.tree.map(lambda a, b: jnp.where(reached, a, b), new, before)  113 us
    dynamic_update_slice x44, local copies, waits for them, and re-layouts, ssd_blocks(): lax.scan(block_step, state_in, (to_blocks(x_heads), to_blocks(b_float), t...  89 us
    reduce_scatter x1, waiting for transfers between devices, per_device(): lax.psum_scatter(lax.dot_general(normed, grad_rows, (((0,), (0,)), ((), (...  48.3 us
    dot_general x6, matrix products, block_step(): y_blk = jnp.einsum('ijh,jhp->ihp', mixing, x_blk, precision=highest)  48.3 us
    all_gather x1, blocking collectives, prefix(): everything = jax.tree.map(lambda part: lax.all_gather(part, axis), shard)  24 us
    mul x2, other arithmetic, block_step(): mixing = gram_mat[:, :, None] * decay_mat * step_blk[None, :, :]  22.6 us
  transfers between devices with their start and end apart: 4, of which 3 were waited for; matrix products, arithmetic and copies ran while one was open for 26% of the time, Pallas kernels for 0%

profile of v1, /device:TPU:1, one launch (start us, length us, event | category | flops | bytes accessed | tf_op | source)
XLA Modules:
  0.0 1044.1 jit_solution(6420701765702877311)
XLA Ops:
  17.8 3.7 copy.144
  21.5 4.1 convert_multiply_fusion
  25.6 3.6 copy.145
  29.2 4.5 fusion.162
  34.0 3.1 copy.147
  37.1 5.3 reshape.1003
  42.5 4.0 copy.148
  46.5 3.2 copy.152
  49.7 5.5 reshape.1008
  55.9 24.0 %all-gather.2 = f32[32,1,48]{2,1,0:T(1,128)S(1)} all-gather(f32[1,1,48]{2,1,0:T(1,128)S(1)} %bitcast.581), channel_id=1, replica_groups=mesh['dp'=4,'seq'=32] {'seq'}, dimensions={0}, use_global_device_ids=true | all-gather | bytes 6336 | tf_op jit(solution)/shard_map/all_gather | solution.py:12
  79.9 115.2 %all-gather.6.cloned.1.call-done = f32[1536,64,128]{2,1,0:T(8,128)} async-done(((f32[48,64,128]{2,1,0:T(8,128)}), f32[1536,64,128]{2,1,0:T(8,128)}) %all-gather.6.cloned.1.call-update) | async-done | bytes 50331664 | tf_op jit(solution)/shard_map/all_gather | solution.py:12
  195.1 58.0 %while.116 = (s32[]{:T(128)}, f32[48,64,128]{2,1,0:T(8,128)S(1)}, s32[]{:T(128)}, f32[32,48]{1,0:T(8,128)S(1)}, f32[32,48,64,128]{3,2,1,0:T(8,128)}, /*index=5*/s32[]{:T(128)}, s32[]{:T(128)}) while((s32[]{:T(128)}, f32[48,64,128]{2,1,0:T(8,128)S(1)}, s32[]{:T(128)}, f32[32,48]{1,0:T(8,128)S(1)}, f32[32,48,64,128]{3,2,1,0:T(8,128)}, ...), condition=%wide.region_6.7_spmd.clone, body=%wide.region_5.6_spmd.clone.sunk | while | flops 1572868 | bytes 4719273 | solution.py:25
  259.2 154.5 %while.115 = (s32[]{:T(128)}, f32[48,64,128]{2,1,0:T(8,128)S(1)}, f32[2,128,48,64]{1,3,2,0:T(8,128)}, pred[2,128,128,48]{2,1,3,0:T(32,128)(4,1)}, f32[2,128,128,...) while((s32[]{:T(128)}, f32[48,64,128]{2,1,0:T(8,128)S(1)}, ...), condition=%wide.region_10.11_spmd.clone, body=%wide.region_7.10_spmd.clone.sunk | while | flops 1848273152 | bytes 111490832 | solution.py:66
  262.9 11.3 %broadcast_multiply_fusion.4 = (f32[1,128,128,48]{3,2,1,0:T(8,128)}, f32[1,128,128,48]{3,2,1,0:T(8,128)}, f32[1,128,128,48]{3,2,1,0:T(8,128)}, f32[1,128,128,48]{3,2,1,0:T(8,128)}) fusion(f32[128,48]{1,0:T(8,128)S(1)} %get-tuple-element.2454, f32[128,48]{1,0:T(8,128)S(1)} %reduce_window_sum.92, pred[128,128]{1,0:T(8,128)(4,1)S(1)} %fusion.251, ...), kind=kLoop, calls=%fused_computation.99.clone.1 | loop fusion | flops 3932160 | bytes 12713984 | tf_op jit(solution)/shard_map/jvp()/while/body/eval_jaxpr/mul | solution.py:39
  274.2 6.9 copy.272
  281.1 6.8 copy.273
  287.9 6.3 constant_dynamic-update-slice_fusion.23
  294.2 6.9 copy.269
  301.1 6.8 copy.270
  307.9 6.4 constant_dynamic-update-slice_fusion.21
  317.1 7.6 bitcast_dynamic-update-slice_fusion.13
  324.7 2.9 multiply_dynamic-update-slice_fusion.2
  339.9 11.3 %broadcast_multiply_fusion.4 = (f32[1,128,128,48]{3,2,1,0:T(8,128)}, f32[1,128,128,48]{3,2,1,0:T(8,128)}, f32[1,128,128,48]{3,2,1,0:T(8,128)}, f32[1,128,128,48]{3,2,1,0:T(8,128)}) fusion(f32[128,48]{1,0:T(8,128)S(1)} %get-tuple-element.2454, f32[128,48]{1,0:T(8,128)S(1)} %reduce_window_sum.92, pred[128,128]{1,0:T(8,128)(4,1)S(1)} %fusion.251, ...), kind=kLoop, calls=%fused_computation.99.clone.1 | loop fusion | flops 3932160 | bytes 12713984 | tf_op jit(solution)/shard_map/jvp()/while/body/eval_jaxpr/mul | solution.py:39
  351.2 6.9 copy.272
  358.1 6.8 copy.273
  365.0 6.3 constant_dynamic-update-slice_fusion.23
  371.2 6.9 copy.269
  378.1 6.8 copy.270
  384.9 6.4 constant_dynamic-update-slice_fusion.21
  391.6 2.6 bitcast_dynamic-update-slice_fusion.11
  394.2 7.6 bitcast_dynamic-update-slice_fusion.13
  401.8 2.9 multiply_dynamic-update-slice_fusion.2
  413.7 7.7 multiply_reduce_fusion.2
  421.4 3.9 multiply_convert_fusion
  425.3 7.8 fusion.146
  436.0 3.6 copy.153
  439.6 6.5 copy.180
  446.1 6.4 reshape.1022
  452.5 10.8 %multiply_reduce_fusion = (f32[3072]{0:T(1024)}, f32[256]{0:T(256)S(1)}, f32[256,3072]{1,0:T(8,128)S(1)}) fusion(f32[256]{0:T(256)S(1)} %bitcast_rsqrt_fusion, bf16[1,256,3072]{2,1,0:T(8,128)(2,1)} %param.21, f32[256,3072]{1,0:T(8,128)} %reshape.1022, f32[3072]{0:T(1024)S(1)} %mul.708, bf16[1,256,3072]{2,1,0:T(8,128)(2,1)S(1)} %copy-done.8, ...), kind=kOutput, calls=%fused_computation.207 | convolution fusion | flops 2427712256 | bytes 19699712 | tf_op jit(solution)/shard_map/dot_general | solution.py:160
  463.3 3.9 fusion.142
  471.0 4.1 copy.154
  475.1 4.6 fusion.160
  480.5 6.1 reshape.1023
  486.6 7.1 copy.158
  494.4 10.0 fusion.143
  504.3 48.3 %reduce-scatter.2.cloned.1.call-done = f32[96,1536]{1,0:T(8,128)} async-done(((f32[3072,1536]{1,0:T(8,128)}), f32[96,1536]{1,0:T(8,128)}) %reduce-scatter.2.cloned.1.call-update) | async-done | bytes 589840 | tf_op jit(solution)/shard_map/reduce_scatter | solution.py:172
  552.7 161.2 %all-gather.8.cloned.1.call-done = f32[1536,64,128]{2,1,0:T(8,128)} async-done(((f32[48,64,128]{2,1,0:T(8,128)}), f32[1536,64,128]{2,1,0:T(8,128)}) %all-gather.8.cloned.1.call-update) | async-done | bytes 50331664 | tf_op jit(solution)/shard_map/all_gather | solution.py:12
  713.8 79.9 %while.117 = (s32[]{:T(128)}, f32[48,64,128]{2,1,0:T(8,128)S(1)}, s32[]{:T(128)}, f32[32,48]{1,0:T(8,128)}, f32[32,48,64,128]{3,2,1,0:T(8,128)}, /*index=5*/s32[]{:T(128)}, s32[]{:T(128)}, s32[]{:T(128)}, s32[]{:T(128)}) while((s32[]{:T(128)}, f32[48,64,128]{2,1,0:T(8,128)S(1)}, s32[]{:T(128)}, f32[32,48]{1,0:T(8,128)}, ...), condition=%wide.region_14.15_spmd.clone, body=%wide.region_13.14_spmd.clone.sunk | while | flops 1572872 | bytes 4719335 | solution.py:25
  797.9 83.0 %while.114 = (s32[]{:T(128)}, f32[48,64,128]{2,1,0:T(8,128)S(1)}, f32[2,128,48,64]{1,3,2,0:T(8,128)}, bf16[2,128,128]{2,1,0:T(8,128)(2,1)}, bf16[2,128,128]{2,1,...) while((s32[]{:T(128)}, f32[48,64,128]{2,1,0:T(8,128)S(1)}, ...), condition=%wide.region_25.26_spmd, body=%wide.region_15.25_spmd.sunk | while | flops 3688450048 | bytes 77251128 | solution.py:66
  798.9 11.1 %fusion.235 = (f32[128,48]{0,1:T(8,128)S(1)}, f32[128,48]{0,1:T(8,128)S(1)}, f32[128,128]{1,0:T(8,128)S(1)}, f32[128,48]{0,1:T(8,128)S(1)}) fusion(f32[2,128,128,48]{2,1,3,0:T(8,128)} %get-tuple-element.2732, s32[]{:T(128)S(6)} %sub.274, f32[128,48]{0,1:T(8,128)S(1)} %dynamic-slice_bitcast_fusion.18, ...), kind=kOutput, calls=%fused_computation.91.clone.1 | convolution fusion | flops 612595712 | bytes 13600256 | tf_op jit(solution)/shard_map/transpose(jvp())/while/body/eval_jaxpr/ijh,jhp->ihp/dot_general | solution.py:40
  812.0 4.0 fusion.233
  821.9 4.7 fusion.237
  827.4 4.0 fusion.234
  831.8 5.5 bitcast_dynamic-update-slice_fusion.10
  840.2 11.1 %fusion.235 = (f32[128,48]{0,1:T(8,128)S(1)}, f32[128,48]{0,1:T(8,128)S(1)}, f32[128,128]{1,0:T(8,128)S(1)}, f32[128,48]{0,1:T(8,128)S(1)}) fusion(f32[2,128,128,48]{2,1,3,0:T(8,128)} %get-tuple-element.2732, s32[]{:T(128)S(6)} %sub.274, f32[128,48]{0,1:T(8,128)S(1)} %dynamic-slice_bitcast_fusion.18, ...), kind=kOutput, calls=%fused_computation.91.clone.1 | convolution fusion | flops 612595712 | bytes 13600256 | tf_op jit(solution)/shard_map/transpose(jvp())/while/body/eval_jaxpr/ijh,jhp->ihp/dot_general | solution.py:40
  853.3 4.0 fusion.233
  863.2 4.7 fusion.237
  868.8 4.0 fusion.234
  873.2 5.4 bitcast_dynamic-update-slice_fusion.10
  883.0 6.1 copy.183
  889.1 5.8 reshape.1024
  895.7 13.0 %all-reduce.3 = (f32[48]{0:T(128)S(1)}, f32[48]{0:T(128)S(1)}, f32[48]{0:T(128)S(1)}, f32[3072]{0:T(1024)S(1)}) all-reduce(f32[48]{0:T(128)S(1)} %get-tuple-element.1778, f32[48]{0:T(128)S(1)} %neg.49, f32[48]{0:T(128)S(1)} %copy-done.36, f32[3072]{0:T(1024)S(1)} %copy-done.32), channel_id=1, replica_groups=mesh['dp'=4,'seq'=32] {'dp'}, use_global_device_ids=true, to_apply=%region_27.28 | all-reduce | flops 3216 | bytes 25728 | tf_op jit(solution)/shard_map/psum | solution.py:170
  908.7 122.1 %all-reduce.2 = (f32[48]{0:T(128)}, f32[48]{0:T(128)}, f32[48]{0:T(128)}, f32[3072]{0:T(1024)}) all-reduce(f32[48]{0:T(128)S(1)} %get-tuple-element.1927, f32[48]{0:T(128)S(1)} %get-tuple-element.1928, f32[48]{0:T(128)S(1)} %get-tuple-element.1929, f32[3072]{0:T(1024)S(1)} %get-tuple-element.1930), channel_id=1, replica_groups=mesh['dp'=4,'seq'=32] {'seq'}, use_global_device_ids=true, to_apply=%region_28.29 | all-reduce | flops 3216 | bytes 25728 | tf_op jit(solution)/shard_map/psum | solution.py:169
  1030.8 4.6 fusion.145
  (450 shorter events, 219.7 us)
Async XLA Ops:
  7.2 418.2 %copy-start = (bf16[1,256,1536]{2,1,0:T(8,128)(2,1)S(1)}, bf16[1,256,1536]{2,1,0:T(8,128)(2,1)}, u32[]{:S(2)}) copy-start(bf16[1,256,1536]{2,1,0:T(8,128)(2,1)} %param.31) | copy-start | bytes 2359300
  7.2 187.9 %all-gather.6.cloned.1.call-start = ((), (), s32[]{:S(2)}) async-start(), calls=%async_computation.3 | async-start | bytes 51904512 | tf_op jit(solution)/shard_map/all_gather | solution.py:12
  12.5 67.4 %copy-start.33 = (f32[48]{0:T(128)}, f32[48]{0:T(128)S(1)}, u32[]{:S(2)}) copy-start(f32[48]{0:T(128)S(1)} %neg.43) | copy-start | bytes 580
  17.8 3.7 copy-start.7
  25.6 3.6 copy-start.16
  29.2 4.6 copy-start.14
  33.8 518.9 %reduce-scatter.2.cloned.1.call-start = ((), (), s32[]{:S(2)}) async-start(), calls=%async_computation.1 | async-start | bytes 19464192 | tf_op jit(solution)/shard_map/reduce_scatter | solution.py:172
  33.9 45.9 %copy-start.12 = (f32[1,256,48]{2,1,0:T(8,128)}, f32[1,256,48]{2,1,0:T(8,128)S(1)}, u32[]{:S(2)}) copy-start(f32[1,256,48]{2,1,0:T(8,128)S(1)} %copy.179) | copy-start | bytes 147460
  42.5 4.0 copy-start.17
  49.7 5.5 copy-start.26
  49.7 30.2 %copy-start.29 = (f32[48]{0:T(128)S(1)}, f32[48]{0:T(128)}, u32[]{:S(2)}) copy-start(f32[48]{0:T(128)} %param.25) | copy-start | bytes 580
  253.1 4.1 copy-start.28
  314.5 2.6 copy-start.2
  328.3 2.5 copy-start.3
  330.7 3.5 copy-start.21
  330.7 3.5 copy-start.40
  330.7 3.6 copy-start.31
  330.7 3.6 copy-start.37
  330.8 4.9 copy-start.43
  334.3 2.2 copy-start.22
  334.3 2.1 copy-start.41
  334.4 2.1 copy-start.38
  335.7 0.7 copy-start.44
  391.6 2.6 copy-start.2
  405.3 2.5 copy-start.3
  407.8 3.5 copy-start.21
  407.8 3.5 copy-start.40
  407.8 3.5 copy-start.31
  407.8 3.6 copy-start.37
  407.8 4.9 copy-start.43
  411.3 2.2 copy-start.22
  411.3 2.1 copy-start.41
  411.4 2.1 copy-start.38
  413.7 7.7 copy-start.20
  433.1 0.8 copy-start.19
  433.2 280.7 %all-gather.8.cloned.1.call-start = ((), (), s32[]{:S(2)}) async-start(), calls=%async_computation.4 | async-start | bytes 51904512 | tf_op jit(solution)/shard_map/all_gather | solution.py:12
  446.1 6.4 copy-start.8
  446.1 6.4 copy-start.27
  452.5 10.8 %copy-start.10 = (f32[256,3072]{1,0:T(8,128)S(1)}, f32[256,3072]{1,0:T(8,128)}, u32[]{:S(2)}) copy-start(f32[256,3072]{1,0:T(8,128)} %reshape.1022) | copy-start | bytes 9437188
  452.5 10.8 %copy-start.11 = (bf16[1,256,3072]{2,1,0:T(8,128)(2,1)S(1)}, bf16[1,256,3072]{2,1,0:T(8,128)(2,1)}, u32[]{:S(2)}) copy-start(bf16[1,256,3072]{2,1,0:T(8,128)(2,1)} %param.21) | copy-start | bytes 4718596
  463.3 5.6 copy-start.9
  467.2 1.6 copy-start.6
  471.0 4.1 copy-start.18
  479.8 555.6 %all-reduce.6.cloned.1.call-start = ((), (), s32[]{:S(2)}) async-start(), calls=%async_computation.2 | async-start | bytes 1179648 | tf_op jit(solution)/shard_map/psum | solution.py:180
  793.7 4.2 copy-start.23
  793.7 4.1 copy-start.39
  793.7 4.1 copy-start.42
  793.7 4.1 copy-start.45
  797.9 84.8 %copy-start.13 = (f32[1,256,48]{2,1,0:T(8,128)S(1)}, f32[1,256,48]{2,1,0:T(8,128)}, u32[]{:S(2)}) copy-start(f32[1,256,48]{2,1,0:T(8,128)} %copy-done.12) | copy-start | bytes 147460
  797.9 84.8 %copy-start.30 = (f32[48]{0:T(128)S(1)}, f32[48]{0:T(128)}, u32[]{:S(2)}) copy-start(f32[48]{0:T(128)} %param.25) | copy-start | bytes 580
  797.9 84.8 %copy-start.34 = (f32[48]{0:T(128)S(1)}, f32[48]{0:T(128)}, u32[]{:S(2)}) copy-start(f32[48]{0:T(128)} %copy-done.33) | copy-start | bytes 580
  798.9 11.2 %copy-start.5 = (f32[2,48,64,128]{3,2,1,0:T(8,128)S(1)}, f32[2,48,64,128]{3,2,1,0:T(8,128)}, u32[]{:S(2)}) copy-start(f32[2,48,64,128]{3,2,1,0:T(8,128)} %get-tuple-element.2719) | copy-start | bytes 9437188 | tf_op jit(solution)/shard_map/transpose(jvp())/while
  821.9 9.6 copy-start.24
  821.9 9.9 copy-start.1
  821.9 9.9 copy-start.4
  831.8 5.5 copy-start.25
  840.2 11.2 %copy-start.5 = (f32[2,48,64,128]{3,2,1,0:T(8,128)S(1)}, f32[2,48,64,128]{3,2,1,0:T(8,128)}, u32[]{:S(2)}) copy-start(f32[2,48,64,128]{3,2,1,0:T(8,128)} %get-tuple-element.2719) | copy-start | bytes 9437188 | tf_op jit(solution)/shard_map/transpose(jvp())/while
  863.2 9.6 copy-start.24
  863.2 9.9 copy-start.1
  863.2 9.9 copy-start.4
  873.1 5.4 copy-start.25
  889.1 5.9 copy-start.15
  889.1 6.6 copy-start.32
  889.1 6.6 copy-start.36
  (2 other events, 1.4 us)
Sparse Core Ops, SparseCore 0:
  33.9 161.1 all-gather.5
  433.3 119.3 reduce-scatter.1
  555.8 158.0 all-gather.7
  716.2 40.1 all-reduce.5
